TPU v7x, 32 devices: a whole 2x2x4 slice. The times are simulated.
32 devices in a mesh: col: 1, row: 32 (over z, y, x, core).
Axes of the slice: x: 2, y: 2, z: 4, core: 2. Of those that a mesh axis runs over, the one named last changes fastest.
Arguments:
- tokens: bfloat16 [128, 8192], P('col', 'row'), may hold values from -6 to 6
- gate_weight: bfloat16 [8192, 14336], P('col', 'row'), may hold values from -0.0625 to 0.0625
- up_weight: bfloat16 [8192, 14336], P('col', 'row'), may hold values from -0.0625 to 0.0625
Outputs:
- hidden: bfloat16 [128, 14336], P('col', 'row')
All inputs are finite; a program needn't handle non-finite values.
Results may differ from a plain program's by a relative error of at most 0.0012.
Values may be sent and summed in bfloat16 or wider, within the bound.
A program may use at most 64 MiB of HBM per device.

v0:
```python
import jax
import jax.numpy as jnp
from jax import lax
from jax.sharding import PartitionSpec as P


def add_block(whole, pieces):
    gate_part = jnp.dot(whole, pieces[0], preferred_element_type=jnp.float32)
    up_part = jnp.dot(whole, pieces[1], preferred_element_type=jnp.float32)
    return (gate_part, up_part)


def local(tokens, gate_weight, up_weight):
    whole = lax.all_gather(tokens, "row", axis=1, tiled=True)
    gate, up = add_block(
        whole,
        (
            lax.all_gather(gate_weight, "col", axis=0, tiled=True),
            lax.all_gather(up_weight, "col", axis=0, tiled=True),
        ),
    )
    return (jax.nn.silu(gate) * up).astype(jnp.bfloat16)


def solution(mesh):
    in_specs = (P("col", "row"), P("col", "row"), P("col", "row"))
    out_specs = P("col", "row")
    return jax.shard_map(local, mesh=mesh, in_specs=in_specs, out_specs=out_specs, check_vma=False)
```

profile of v0, /device:TPU:0, one launch (start us, length us, event | category | flops | bytes accessed | tf_op | source)
XLA Modules:
  0.0 85.6 jit_solution(13650181281954059756)
XLA Ops:
  6.5 0.0 all-gather.2.cloned.1.call-start
  6.5 0.7 all-gather.2.cloned.1.call-update
  7.3 62.4 %all-gather.2.cloned.1.call-done = bf16[128,8192]{1,0:T(8,128)(2,1)} async-done(((bf16[128,256]{1,0:T(8,128)(2,1)}), bf16[128,8192]{1,0:T(8,128)(2,1)}) %all-gather.2.cloned.1.call-update) | async-done | bytes 2097168 | tf_op jit(solution)/shard_map/all_gather | solution.py:14
  69.6 0.0 copy-start
  69.6 0.0 copy-start.1
  69.6 5.9 %fusion.1 = f32[128,448]{0,1:T(8,128)S(1)} fusion(bf16[128,8192]{1,0:T(8,128)(2,1)} %all-gather.2.cloned.1.call-done, bf16[8192,448]{0,1:T(8,128)(2,1)} %param.4), kind=kOutput, calls=%fused_computation.2 | convolution fusion | flops 939524096 | bytes 9666560 | tf_op jit(solution)/shard_map/dot_general | solution.py:8
  75.6 0.0 copy-done
  75.6 0.5 copy-done.1
  76.1 2.7 %fusion = bf16[128,448]{0,1:T(8,128)(2,1)} fusion(bf16[128,8192]{1,0:T(8,128)(2,1)S(1)} %copy-done, bf16[8192,448]{0,1:T(8,128)(2,1)S(1)} %copy-done.1, f32[128,448]{0,1:T(8,128)S(1)} %fusion.1), kind=kOutput, calls=%fused_computation.1 | convolution fusion | flops 939868160 | bytes 9781248 | tf_op jit(solution)/shard_map/dot_general | solution.py:9
Async XLA Ops:
  6.5 63.1 %all-gather.2.cloned.1.call-start = ((), (), s32[]{:S(2)}) async-start(), calls=%async_computation | async-start | bytes 2162688 | tf_op jit(solution)/shard_map/all_gather | solution.py:14
  69.6 5.9 %copy-start = (bf16[128,8192]{1,0:T(8,128)(2,1)S(1)}, bf16[128,8192]{1,0:T(8,128)(2,1)}, u32[]{:S(2)}) copy-start(bf16[128,8192]{1,0:T(8,128)(2,1)} %all-gather.2.cloned.1.call-done) | copy-start | bytes 6291460
  69.6 6.4 %copy-start.1 = (bf16[8192,448]{0,1:T(8,128)(2,1)S(1)}, bf16[8192,448]{0,1:T(8,128)(2,1)}, u32[]{:S(2)}) copy-start(bf16[8192,448]{0,1:T(8,128)(2,1)} %param.5) | copy-start | bytes 22020100
Sparse Core Ops, SparseCore 0:
  10.2 59.3 all-gather.1
where the time goes:
time: 85.8 us; the launch traced here: 85.6 us
  waiting for transfers between devices  63.1 us (74%)
  between operations  13.4 us (16%)
  matrix products  8.63 us (10%)
    all_gather x1, waiting for transfers between devices, local(): whole = lax.all_gather(tokens, 'row', axis=1, tiled=True)  62.4 us
    dot_general x1, matrix products, add_block(): gate_part = jnp.dot(whole, pieces[0], preferred_element_type=jnp.float32)  5.92 us
    dot_general x1, matrix products, add_block(): up_part = jnp.dot(whole, pieces[1], preferred_element_type=jnp.float32)  2.71 us
  transfers between devices with their start and end apart: 1, of which 1 were waited for; matrix products, arithmetic and copies ran while one was open for 0% of the time, Pallas kernels for 0%

commit v1 on v0

v1 whole, which is shorter than its diff:
```python
import functools

import jax
import jax.numpy as jnp
from jax import lax
from jax.experimental import pallas as pl
from jax.experimental.pallas import tpu as pltpu
from jax.sharding import PartitionSpec as P

PLANE = 8


def dot_t(a, b):
    return lax.dot_general(a, b, (((1,), (1,)), ((), ())), preferred_element_type=jnp.float32)


def kernel(planes, tok_hbm, gate_hbm, up_hbm, out_ref, tok, gate_w, up_w, gate_acc, up_acc,
           own_sem, w_sem, send_sem, recv_sem):
    me = lax.axis_index("row")
    z = me // PLANE
    spot = me % PLANE
    core = me % 2
    x = (me // 2) % 2
    y = (me // 4) % 2
    deep = gate_hbm.shape[1] // planes
    pair = deep // (PLANE // 2)

    step_x = 2 - 4 * x
    step_y = 4 - 8 * y
    step_a = step_x + core * (step_y - step_x)
    step_b = step_y + core * (step_x - step_y)
    to_a = me + step_a
    to_b = me + step_b
    sibling = me + 1 - 2 * core

    half = z // (planes // 2)
    low = z + half * (planes - 1 - 2 * z)
    zs = [z]
    for k in range(1, planes):
        f = k - low if k == 1 else k
        zs.append(f + half * (planes - 1 - 2 * f))

    own = pltpu.make_async_copy(tok_hbm, tok.at[me], own_sem)
    own.start()

    barrier = pltpu.get_barrier_semaphore()
    partners = [zk * PLANE + spot for zk in zs[1:]] + [to_a, to_b, sibling]
    for other in partners:
        pl.semaphore_signal(barrier, inc=1, device_id={"row": other}, device_id_type=pl.DeviceIdType.MESH)

    weights = []
    for k, zk in enumerate(zs):
        rows = pl.ds(pl.multiple_of(zk * deep, deep), deep)
        pieces = [
            pltpu.make_async_copy(gate_hbm.at[:, rows], gate_w.at[:, rows], w_sem.at[k, 0]),
            pltpu.make_async_copy(up_hbm.at[:, rows], up_w.at[:, rows], w_sem.at[k, 1]),
        ]
        weights.append(pieces)

    for piece in weights[0]:
        piece.start()
    own.wait()
    pl.semaphore_wait(barrier, len(partners))

    sends = []

    def send(block, other):
        copy = pltpu.make_async_remote_copy(
            src_ref=tok.at[block],
            dst_ref=tok.at[block],
            send_sem=send_sem.at[len(sends)],
            recv_sem=recv_sem.at[block],
            device_id={"row": other},
            device_id_type=pl.DeviceIdType.MESH,
        )
        copy.start()
        sends.append(copy)

    def arrived(block):
        pltpu.make_async_remote_copy(
            src_ref=tok.at[block],
            dst_ref=tok.at[block],
            send_sem=send_sem.at[0],
            recv_sem=recv_sem.at[block],
            device_id={"row": sibling},
            device_id_type=pl.DeviceIdType.MESH,
        ).wait_recv()

    moves = {"L": 0, "A": step_a, "B": step_b, "AB": step_a + step_b}

    def block_of(kind, k):
        return zs[k] * PLANE + spot + moves[kind]

    def event(kind, k):
        block = block_of(kind, k)
        if kind != "L" or k:
            arrived(block)
        if kind == "L":
            send(block, to_a)
            send(block, to_b)
        if kind == "A":
            send(block, to_b)
        send(block, sibling)

    def compute(kind, k):
        block = block_of(kind, k)
        arrived(block + 1 - 2 * core)
        chip = block // 2
        rows = pl.ds(pl.multiple_of(chip * pair, pair), pair)
        part = jnp.concatenate([tok[2 * chip], tok[2 * chip + 1]], axis=1)
        gate = dot_t(gate_w[:, rows], part)
        up = dot_t(up_w[:, rows], part)
        if kind == "L" and k == 0:
            gate_acc[...] = gate
            up_acc[...] = up
        else:
            gate_acc[...] += gate
            up_acc[...] += up

    for zk in zs[:0:-1]:
        send(me, zk * PLANE + spot)
    event("L", 0)
    for group in weights[1:]:
        for piece in group:
            piece.start()

    order = [
        ("A", 0), ("L", 1), ("B", 0), ("AB", 0), ("A", 1), "w0", "L0", ("L", 2), "A0", ("B", 1), "B0", ("AB", 1),
        "AB0", ("A", 2), "w1", "L1", ("L", 3), "A1", ("B", 2), "B1", ("AB", 2), "AB1", ("A", 3),
        "w2", "L2", "A2", ("B", 3), "B2", "AB2", "w3", "L3", ("AB", 3), "A3", "B3", "AB3",
    ]
    for item in order:
        if isinstance(item, tuple):
            event(*item)
        elif item[0] == "w":
            for piece in weights[int(item[1])]:
                piece.wait()
        else:
            compute(item[:-1], int(item[-1]))

    gate = gate_acc[...]
    out_ref[...] = (gate / (1.0 + jnp.exp(-gate)) * up_acc[...]).astype(out_ref.dtype)
    for copy in sends:
        copy.wait_send()


def fused(parts, tokens, gate_weight, up_weight):
    planes = parts // PLANE
    rows, columns = tokens.shape[0], gate_weight.shape[0]
    return pl.pallas_call(
        functools.partial(kernel, planes),
        out_shape=jax.ShapeDtypeStruct((columns, rows), jnp.bfloat16),
        in_specs=[pl.BlockSpec(memory_space=pl.ANY)] * 3,
        out_specs=pl.BlockSpec(memory_space=pltpu.VMEM),
        scratch_shapes=[
            pltpu.VMEM((parts,) + tokens.shape, tokens.dtype),
            pltpu.VMEM(gate_weight.shape, gate_weight.dtype),
            pltpu.VMEM(up_weight.shape, up_weight.dtype),
            pltpu.VMEM((columns, rows), jnp.float32),
            pltpu.VMEM((columns, rows), jnp.float32),
            pltpu.SemaphoreType.DMA,
            pltpu.SemaphoreType.DMA((planes, 2)),
            pltpu.SemaphoreType.DMA((parts,)),
            pltpu.SemaphoreType.DMA((parts,)),
        ],
        compiler_params=pltpu.CompilerParams(
            collective_id=0, has_side_effects=True, vmem_limit_bytes=56 * 1024 * 1024
        ),
        cost_estimate=pl.CostEstimate(
            flops=4 * rows * gate_weight.size,
            bytes_accessed=4 * gate_weight.size,
            transcendentals=rows * columns,
        ),
    )(tokens, gate_weight, up_weight)


def local(mesh, tokens, gate_weight, up_weight):
    if mesh.shape["col"] > 1:
        gate_weight = lax.all_gather(gate_weight, "col", axis=0, tiled=True)
        up_weight = lax.all_gather(up_weight, "col", axis=0, tiled=True)
    parts = mesh.shape["row"]
    if parts == 4 * PLANE:
        return fused(parts, tokens, gate_weight.T, up_weight.T).T
    whole = lax.all_gather(tokens, "row", axis=1, tiled=True)
    gate = jnp.dot(whole, gate_weight, preferred_element_type=jnp.float32)
    up = jnp.dot(whole, up_weight, preferred_element_type=jnp.float32)
    return (jax.nn.silu(gate) * up).astype(jnp.bfloat16)


def solution(mesh):
    spec = P("col", "row")
    return jax.shard_map(
        functools.partial(local, mesh), mesh=mesh, in_specs=(spec, spec, spec), out_specs=spec, check_vma=False
    )
```

time: 85.8 us -> 29.5 us (0.34)
  waiting for transfers between devices: 63.1 us -> 0 us
  Pallas kernels: 0 us -> 27.6 us
  between operations: 13.4 us -> 0.01 us
  matrix products: 8.63 us -> 0 us
  local copies, waits for them, and re-layouts: 0.51 us -> 1.55 us
    all_gather x1 -> x0, waiting for transfers between devices: 62.4 us -> none  [local(): whole = lax.all_gather(tokens, 'row', axis=1, tiled=True)]
    pallas_call x0 -> x1, Pallas kernels: none -> 27.6 us  [fused(): pl.pallas_call(functools.partial(kernel, planes), out_shape=jax.ShapeDtyp...]
    dot_general x2 -> x0, matrix products: 8.63 us -> none  [the longest x1 5.92 us: add_block(): gate_part = jnp.dot(whole, pieces[0], preferred_element_type=jnp.float32)]
    unnamed x4 -> x1, local copies, waits for them, and re-layouts: 0.51 us -> 1.55 us
  transfers between devices with their start and end apart: 1 -> 0, of which waited for: 1 -> 0; matrix products, arithmetic and copies ran while one was open for 0% -> 0% of each run, Pallas kernels for 0% -> 0%
where the time goes in v1:
time: 29.5 us; the launch traced here: 29.2 us
  Pallas kernels  27.6 us (94%)
  local copies, waits for them, and re-layouts  1.55 us (5%)
    pallas_call x1, Pallas kernels, fused(): pl.pallas_call(functools.partial(kernel, planes), out_shape=jax.ShapeDtyp...  27.6 us
    unnamed x1, local copies, waits for them, and re-layouts  1.55 us

profile of v1, /device:TPU:0, one launch (start us, length us, event | category | flops | bytes accessed | tf_op | source)
XLA Modules:
  0.0 29.2 jit_solution(7551331089462593943)
XLA Ops:
  0.0 27.6 %shard_map.37 = bf16[448,128]{1,0:T(8,128)(2,1)} custom-call(bf16[128,256]{1,0:T(8,128)(2,1)} %tok_hbm.1, bf16[448,8192]{1,0:T(8,128)(2,1)} %bitcast.3, bf16[448,8192]{1,0:T(8,128)(2,1)} %bitcast.4), custom_call_target="tpu_custom_call" | custom-call | flops 1879048192 | bytes 14680064 | tf_op jit(solution)/shard_map/pallas_call | solution.py:150
  27.7 1.6 %copy.5 = bf16[128,448]{0,1:T(8,128)(2,1)} copy(bf16[128,448]{0,1:T(8,128)(2,1)} %bitcast.5) | data formatting | bytes 229376

commit v2 on v1

--- a/solution.py
+++ b/solution.py
@@ -14,7 +14,7 @@
     return lax.dot_general(a, b, (((1,), (1,)), ((), ())), preferred_element_type=jnp.float32)
 
 
-def kernel(planes, tok_hbm, gate_hbm, up_hbm, out_ref, tok, gate_w, up_w, gate_acc, up_acc,
+def kernel(planes, tok_hbm, gate_hbm, up_hbm, out_ref, tok, weight, acc,
            own_sem, w_sem, send_sem, recv_sem):
     me = lax.axis_index("row")
     z = me // PLANE
@@ -23,6 +23,7 @@
     x = (me // 2) % 2
     y = (me // 4) % 2
     deep = gate_hbm.shape[1] // planes
+    units = gate_hbm.shape[0]
     pair = deep // (PLANE // 2)
 
     step_x = 2 - 4 * x
@@ -52,8 +53,8 @@
     for k, zk in enumerate(zs):
         rows = pl.ds(pl.multiple_of(zk * deep, deep), deep)
         pieces = [
-            pltpu.make_async_copy(gate_hbm.at[:, rows], gate_w.at[:, rows], w_sem.at[k, 0]),
-            pltpu.make_async_copy(up_hbm.at[:, rows], up_w.at[:, rows], w_sem.at[k, 1]),
+            pltpu.make_async_copy(gate_hbm.at[:, rows], weight.at[pl.ds(0, units), rows], w_sem.at[k, 0]),
+            pltpu.make_async_copy(up_hbm.at[:, rows], weight.at[pl.ds(units, units), rows], w_sem.at[k, 1]),
         ]
         weights.append(pieces)
 
@@ -97,7 +98,12 @@
             arrived(block)
         if kind == "L":
             send(block, to_a)
+            if k == 0:
+                send(block, zs[1] * PLANE + spot)
             send(block, to_b)
+            if k == 0:
+                for zk in zs[2:]:
+                    send(block, zk * PLANE + spot)
         if kind == "A":
             send(block, to_b)
         send(block, sibling)
@@ -108,26 +114,21 @@
         chip = block // 2
         rows = pl.ds(pl.multiple_of(chip * pair, pair), pair)
         part = jnp.concatenate([tok[2 * chip], tok[2 * chip + 1]], axis=1)
-        gate = dot_t(gate_w[:, rows], part)
-        up = dot_t(up_w[:, rows], part)
+        both = dot_t(weight[:, rows], part)
         if kind == "L" and k == 0:
-            gate_acc[...] = gate
-            up_acc[...] = up
+            acc[...] = both
         else:
-            gate_acc[...] += gate
-            up_acc[...] += up
+            acc[...] += both
 
-    for zk in zs[:0:-1]:
-        send(me, zk * PLANE + spot)
     event("L", 0)
     for group in weights[1:]:
         for piece in group:
             piece.start()
 
     order = [
-        ("A", 0), ("L", 1), ("B", 0), ("AB", 0), ("A", 1), "w0", "L0", ("L", 2), "A0", ("B", 1), "B0", ("AB", 1),
-        "AB0", ("A", 2), "w1", "L1", ("L", 3), "A1", ("B", 2), "B1", ("AB", 2), "AB1", ("A", 3),
-        "w2", "L2", "A2", ("B", 3), "B2", "AB2", "w3", "L3", ("AB", 3), "A3", "B3", "AB3",
+        ("A", 0), ("L", 1), ("B", 0), "w0", "L0", ("A", 1), "A0", ("AB", 0), ("L", 2), "B0", ("B", 1), "AB0", ("A", 2),
+        "w1", "L1", ("L", 3), "A1", ("AB", 1), "B1", ("B", 2), "AB1", ("A", 3), "w2", "L2", ("AB", 2), "A2", ("B", 3),
+        "B2", "AB2", "w3", "L3", ("AB", 3), "A3", "B3", "AB3",
     ]
     for item in order:
         if isinstance(item, tuple):
@@ -138,8 +139,8 @@
         else:
             compute(item[:-1], int(item[-1]))
 
-    gate = gate_acc[...]
-    out_ref[...] = (gate / (1.0 + jnp.exp(-gate)) * up_acc[...]).astype(out_ref.dtype)
+    gate = acc[pl.ds(0, units), :]
+    out_ref[...] = (gate / (1.0 + jnp.exp(-gate)) * acc[pl.ds(units, units), :]).astype(out_ref.dtype)
     for copy in sends:
         copy.wait_send()
 
@@ -154,10 +155,8 @@
         out_specs=pl.BlockSpec(memory_space=pltpu.VMEM),
         scratch_shapes=[
             pltpu.VMEM((parts,) + tokens.shape, tokens.dtype),
-            pltpu.VMEM(gate_weight.shape, gate_weight.dtype),
-            pltpu.VMEM(up_weight.shape, up_weight.dtype),
-            pltpu.VMEM((columns, rows), jnp.float32),
-            pltpu.VMEM((columns, rows), jnp.float32),
+            pltpu.VMEM((2 * columns, gate_weight.shape[1]), gate_weight.dtype),
+            pltpu.VMEM((2 * columns, rows), jnp.float32),
             pltpu.SemaphoreType.DMA,
             pltpu.SemaphoreType.DMA((planes, 2)),
             pltpu.SemaphoreType.DMA((parts,)),

time: 29.5 us -> 27.8 us (0.942)
  Pallas kernels: 27.6 us -> 26.1 us
    pallas_call x1, Pallas kernels: 27.6 us -> 26.1 us  [fused(): pl.pallas_call(functools.partial(kernel, planes), out_shape=jax.ShapeDtyp...]
where the time goes in v2:
time: 27.8 us; the launch traced here: 27.7 us
  Pallas kernels  26.1 us (94%)
  local copies, waits for them, and re-layouts  1.55 us (6%)
    pallas_call x1, Pallas kernels, fused(): pl.pallas_call(functools.partial(kernel, planes), out_shape=jax.ShapeDtyp...  26.1 us
    unnamed x1, local copies, waits for them, and re-layouts  1.55 us

profile of v2, /device:TPU:0, one launch (start us, length us, event | category | flops | bytes accessed | tf_op | source)
XLA Modules:
  0.0 27.7 jit_solution(870546076191655438)
XLA Ops:
  0.0 26.1 %shard_map.37 = bf16[448,128]{1,0:T(8,128)(2,1)} custom-call(bf16[128,256]{1,0:T(8,128)(2,1)} %tok_hbm.1, bf16[448,8192]{1,0:T(8,128)(2,1)} %bitcast.3, bf16[448,8192]{1,0:T(8,128)(2,1)} %bitcast.4), custom_call_target="tpu_custom_call" | custom-call | flops 1879048192 | bytes 14680064 | tf_op jit(solution)/shard_map/pallas_call | solution.py:151
  26.1 1.6 %copy.5 = bf16[128,448]{0,1:T(8,128)(2,1)} copy(bf16[128,448]{0,1:T(8,128)(2,1)} %bitcast.5) | data formatting | bytes 229376

commit v3 on v2

--- a/solution.py
+++ b/solution.py
@@ -58,7 +58,7 @@
         ]
         weights.append(pieces)
 
-    for piece in weights[0]:
+    for piece in weights[0] + weights[1]:
         piece.start()
     own.wait()
     pl.semaphore_wait(barrier, len(partners))
@@ -121,9 +121,7 @@
             acc[...] += both
 
     event("L", 0)
-    for group in weights[1:]:
-        for piece in group:
-            piece.start()
+    later = [piece for group in weights[2:] for piece in group]
 
     order = [
         ("A", 0), ("L", 1), ("B", 0), "w0", "L0", ("A", 1), "A0", ("AB", 0), ("L", 2), "B0", ("B", 1), "AB0", ("A", 2),
@@ -133,6 +131,8 @@
     for item in order:
         if isinstance(item, tuple):
             event(*item)
+            if later:
+                later.pop(0).start()
         elif item[0] == "w":
             for piece in weights[int(item[1])]:
                 piece.wait()

time: 27.8 us -> 27.8 us (level)
  no operation moved by 1% of the time
where the time goes in v3:
time: 27.8 us; the launch traced here: 27.7 us
  Pallas kernels  26.1 us (94%)
  local copies, waits for them, and re-layouts  1.55 us (6%)
    pallas_call x1, Pallas kernels, fused(): pl.pallas_call(functools.partial(kernel, planes), out_shape=jax.ShapeDtyp...  26.1 us
    unnamed x1, local copies, waits for them, and re-layouts  1.55 us

profile of v3, /device:TPU:0, one launch (start us, length us, event | category | flops | bytes accessed | tf_op | source)
XLA Modules:
  0.0 27.7 jit_solution(12373617917926448442)
XLA Ops:
  0.0 26.1 %shard_map.37 = bf16[448,128]{1,0:T(8,128)(2,1)} custom-call(bf16[128,256]{1,0:T(8,128)(2,1)} %tok_hbm.1, bf16[448,8192]{1,0:T(8,128)(2,1)} %bitcast.3, bf16[448,8192]{1,0:T(8,128)(2,1)} %bitcast.4), custom_call_target="tpu_custom_call" | custom-call | flops 1879048192 | bytes 14680064 | tf_op jit(solution)/shard_map/pallas_call | solution.py:151
  26.1 1.6 %copy.5 = bf16[128,448]{0,1:T(8,128)(2,1)} copy(bf16[128,448]{0,1:T(8,128)(2,1)} %bitcast.5) | data formatting | bytes 229376

commit v4 on v2

--- a/solution.py
+++ b/solution.py
@@ -1,4 +1,5 @@
 import functools
+import itertools
 
 import jax
 import jax.numpy as jnp
@@ -63,39 +64,27 @@
     own.wait()
     pl.semaphore_wait(barrier, len(partners))
 
-    sends = []
-
-    def send(block, other):
-        copy = pltpu.make_async_remote_copy(
+    def remote(block, index, other):
+        return pltpu.make_async_remote_copy(
             src_ref=tok.at[block],
             dst_ref=tok.at[block],
-            send_sem=send_sem.at[len(sends)],
+            send_sem=send_sem.at[index],
             recv_sem=recv_sem.at[block],
             device_id={"row": other},
             device_id_type=pl.DeviceIdType.MESH,
         )
-        copy.start()
-        sends.append(copy)
-
-    def arrived(block):
-        pltpu.make_async_remote_copy(
-            src_ref=tok.at[block],
-            dst_ref=tok.at[block],
-            send_sem=send_sem.at[0],
-            recv_sem=recv_sem.at[block],
-            device_id={"row": sibling},
-            device_id_type=pl.DeviceIdType.MESH,
-        ).wait_recv()
-
+
+    count = itertools.count()
     moves = {"L": 0, "A": step_a, "B": step_b, "AB": step_a + step_b}
-
-    def block_of(kind, k):
-        return zs[k] * PLANE + spot + moves[kind]
+    blocks = {(kind, k): zs[k] * PLANE + spot + move for kind, move in moves.items() for k in range(planes)}
+
+    def send(block, other):
+        remote(block, next(count), other).start()
 
     def event(kind, k):
-        block = block_of(kind, k)
+        block = blocks[kind, k]
         if kind != "L" or k:
-            arrived(block)
+            remote(block, 0, sibling).wait_recv()
         if kind == "L":
             send(block, to_a)
             if k == 0:
@@ -108,41 +97,59 @@
             send(block, to_b)
         send(block, sibling)
 
-    def compute(kind, k):
-        block = block_of(kind, k)
-        arrived(block + 1 - 2 * core)
-        chip = block // 2
-        rows = pl.ds(pl.multiple_of(chip * pair, pair), pair)
-        part = jnp.concatenate([tok[2 * chip], tok[2 * chip + 1]], axis=1)
-        both = dot_t(weight[:, rows], part)
-        if kind == "L" and k == 0:
-            acc[...] = both
-        else:
-            acc[...] += both
-
     event("L", 0)
     for group in weights[1:]:
         for piece in group:
             piece.start()
-
-    order = [
-        ("A", 0), ("L", 1), ("B", 0), "w0", "L0", ("A", 1), "A0", ("AB", 0), ("L", 2), "B0", ("B", 1), "AB0", ("A", 2),
-        "w1", "L1", ("L", 3), "A1", ("AB", 1), "B1", ("B", 2), "AB1", ("A", 3), "w2", "L2", ("AB", 2), "A2", ("B", 3),
-        "B2", "AB2", "w3", "L3", ("AB", 3), "A3", "B3", "AB3",
+    acc[...] = jnp.zeros_like(acc)
+
+    steps = [
+        ([("A", 0), ("L", 1), 0], ("L", 0)),
+        ([("B", 0)], ("A", 0)),
+        ([("A", 1), ("AB", 0), ("L", 2)], ("B", 0)),
+        ([("B", 1), 1], ("L", 1)),
+        ([], ("AB", 0)),
+        ([("A", 2)], ("A", 1)),
+        ([("L", 3), ("AB", 1)], ("B", 1)),
+        ([("B", 2)], ("AB", 1)),
+        ([2], ("L", 2)),
+        ([], ("A", 2)),
+        ([("A", 3), ("AB", 2)], ("B", 2)),
+        ([("B", 3)], ("AB", 2)),
+        ([3], ("L", 3)),
+        ([], ("A", 3)),
+        ([("AB", 3)], ("B", 3)),
+        ([], ("AB", 3)),
     ]
-    for item in order:
-        if isinstance(item, tuple):
-            event(*item)
-        elif item[0] == "w":
-            for piece in weights[int(item[1])]:
-                piece.wait()
-        else:
-            compute(item[:-1], int(item[-1]))
+
+    def take(items):
+        for item in items:
+            if isinstance(item, tuple):
+                event(*item)
+            else:
+                for piece in weights[item]:
+                    piece.wait()
+
+    def body(step, carry):
+        block = blocks[steps[0][1]]
+        for at, (items, chip_key) in enumerate(steps):
+            if items:
+                pl.when(step == at)(functools.partial(take, items))
+            if at:
+                block = jnp.where(step == at, blocks[chip_key], block)
+        remote(block + 1 - 2 * core, 0, sibling).wait_recv()
+        chip = block // 2
+        rows = pl.ds(pl.multiple_of(chip * pair, pair), pair)
+        part = jnp.concatenate([tok[2 * chip], tok[2 * chip + 1]], axis=1)
+        acc[...] += dot_t(weight[:, rows], part)
+        return carry
+
+    lax.fori_loop(0, len(steps), body, 0)
 
     gate = acc[pl.ds(0, units), :]
     out_ref[...] = (gate / (1.0 + jnp.exp(-gate)) * acc[pl.ds(units, units), :]).astype(out_ref.dtype)
-    for copy in sends:
-        copy.wait_send()
+    for index in range(next(count)):
+        remote(me, index, sibling).wait_send()
 
 
 def fused(parts, tokens, gate_weight, up_weight):

time: 27.8 us -> 26.9 us (0.968); the launches traced: 27.7 us -> 26.4 us
  Pallas kernels: 26.1 us -> 24.9 us
    pallas_call x1, Pallas kernels: 26.1 us -> 24.9 us  [fused(): pl.pallas_call(functools.partial(kernel, planes), out_shape=jax.ShapeDtyp...]
where the time goes in v4:
time: 26.9 us; the launch traced here: 26.4 us
  Pallas kernels  24.9 us (93%)
  local copies, waits for them, and re-layouts  1.55 us (6%)
    pallas_call x1, Pallas kernels, fused(): pl.pallas_call(functools.partial(kernel, planes), out_shape=jax.ShapeDtyp...  24.9 us
    unnamed x1, local copies, waits for them, and re-layouts  1.55 us

profile of v4, /device:TPU:0, one launch (start us, length us, event | category | flops | bytes accessed | tf_op | source)
XLA Modules:
  0.0 26.4 jit_solution(12659671914081265850)
XLA Ops:
  0.0 24.9 %shard_map.37 = bf16[448,128]{1,0:T(8,128)(2,1)} custom-call(bf16[128,256]{1,0:T(8,128)(2,1)} %tok_hbm.1, bf16[448,8192]{1,0:T(8,128)(2,1)} %bitcast.3, bf16[448,8192]{1,0:T(8,128)(2,1)} %bitcast.4), custom_call_target="tpu_custom_call" | custom-call | flops 1879048192 | bytes 14680064 | tf_op jit(solution)/shard_map/pallas_call | solution.py:158
  24.9 1.6 %copy.5 = bf16[128,448]{0,1:T(8,128)(2,1)} copy(bf16[128,448]{0,1:T(8,128)(2,1)} %bitcast.5) | data formatting | bytes 229376

commit v5 on v4

--- a/solution.py
+++ b/solution.py
@@ -17,6 +17,7 @@
 
 def kernel(planes, tok_hbm, gate_hbm, up_hbm, out_ref, tok, weight, acc,
            own_sem, w_sem, send_sem, recv_sem):
+    parts = planes * PLANE
     me = lax.axis_index("row")
     z = me // PLANE
     spot = me % PLANE
@@ -81,8 +82,46 @@
     def send(block, other):
         remote(block, next(count), other).start()
 
+    def half(block, part, index, arrival, other):
+        rows = pl.ds(part * (tok.shape[1] // 2), tok.shape[1] // 2)
+        return pltpu.make_async_remote_copy(
+            src_ref=tok.at[block, rows],
+            dst_ref=tok.at[block, rows],
+            send_sem=send_sem.at[index],
+            recv_sem=recv_sem.at[arrival],
+            device_id={"row": other},
+            device_id_type=pl.DeviceIdType.MESH,
+        )
+
+    halves = set()
+
+    def next_half():
+        index = next(count)
+        halves.add(index)
+        return index
+
+    last = planes - 1
+
     def event(kind, k):
         block = blocks[kind, k]
+        if k == last and kind in ("A", "AB"):
+            extra = parts if kind == "A" else parts + 1
+            for part, arrival in enumerate((block, extra)):
+                half(block, part, 0, arrival, sibling).wait_recv()
+                if kind == "A":
+                    half(block, part, next_half(), parts + 1 if part else block, to_b).start()
+                else:
+                    half(block, part, next_half(), block, sibling).start()
+            if kind == "A":
+                send(block, sibling)
+            return
+        if k == last and kind == "L":
+            remote(block, 0, sibling).wait_recv()
+            half(block, 0, next_half(), block, to_a).start()
+            half(block, 1, next_half(), parts, to_a).start()
+            send(block, to_b)
+            send(block, sibling)
+            return
         if kind != "L" or k:
             remote(block, 0, sibling).wait_recv()
         if kind == "L":
@@ -149,7 +188,10 @@
     gate = acc[pl.ds(0, units), :]
     out_ref[...] = (gate / (1.0 + jnp.exp(-gate)) * acc[pl.ds(units, units), :]).astype(out_ref.dtype)
     for index in range(next(count)):
-        remote(me, index, sibling).wait_send()
+        if index in halves:
+            half(me, 0, index, 0, sibling).wait_send()
+        else:
+            remote(me, index, sibling).wait_send()
 
 
 def fused(parts, tokens, gate_weight, up_weight):
@@ -166,8 +208,8 @@
             pltpu.VMEM((2 * columns, rows), jnp.float32),
             pltpu.SemaphoreType.DMA,
             pltpu.SemaphoreType.DMA((planes, 2)),
-            pltpu.SemaphoreType.DMA((parts,)),
-            pltpu.SemaphoreType.DMA((parts,)),
+            pltpu.SemaphoreType.DMA((parts + 4,)),
+            pltpu.SemaphoreType.DMA((parts + 2,)),
         ],
         compiler_params=pltpu.CompilerParams(
             collective_id=0, has_side_effects=True, vmem_limit_bytes=56 * 1024 * 1024

time: 26.9 us -> 26.7 us (level); the launches traced: 26.4 us -> 26.5 us
  no operation moved by 1% of the time
where the time goes in v5:
time: 26.7 us; the launch traced here: 26.5 us
  Pallas kernels  25 us (94%)
  local copies, waits for them, and re-layouts  1.55 us (6%)
    pallas_call x1, Pallas kernels, fused(): pl.pallas_call(functools.partial(kernel, planes), out_shape=jax.ShapeDtyp...  25 us
    unnamed x1, local copies, waits for them, and re-layouts  1.55 us

profile of v5, /device:TPU:0, one launch (start us, length us, event | category | flops | bytes accessed | tf_op | source)
XLA Modules:
  0.0 26.5 jit_solution(16051331793494093769)
XLA Ops:
  0.0 25.0 %shard_map.37 = bf16[448,128]{1,0:T(8,128)(2,1)} custom-call(bf16[128,256]{1,0:T(8,128)(2,1)} %tok_hbm.1, bf16[448,8192]{1,0:T(8,128)(2,1)} %bitcast.3, bf16[448,8192]{1,0:T(8,128)(2,1)} %bitcast.4), custom_call_target="tpu_custom_call" | custom-call | flops 1879048192 | bytes 14680064 | tf_op jit(solution)/shard_map/pallas_call | solution.py:200
  25.0 1.6 %copy.5 = bf16[128,448]{0,1:T(8,128)(2,1)} copy(bf16[128,448]{0,1:T(8,128)(2,1)} %bitcast.5) | data formatting | bytes 229376

commit v6 on v5

--- a/solution.py
+++ b/solution.py
@@ -152,12 +152,12 @@
         ([("L", 3), ("AB", 1)], ("B", 1)),
         ([("B", 2)], ("AB", 1)),
         ([2], ("L", 2)),
-        ([], ("A", 2)),
-        ([("A", 3), ("AB", 2)], ("B", 2)),
-        ([("B", 3)], ("AB", 2)),
+        ([("A", 3), ("AB", 2)], ("A", 2)),
+        ([("B", 3)], ("B", 2)),
+        ([], ("AB", 2)),
         ([3], ("L", 3)),
-        ([], ("A", 3)),
-        ([("AB", 3)], ("B", 3)),
+        ([("AB", 3)], ("A", 3)),
+        ([], ("B", 3)),
         ([], ("AB", 3)),
     ]
 

time: 26.7 us -> 26.8 us (level)
  no operation moved by 1% of the time
where the time goes in v6:
time: 26.8 us; the launch traced here: 26.6 us
  Pallas kernels  25.1 us (94%)
  local copies, waits for them, and re-layouts  1.55 us (6%)
    pallas_call x1, Pallas kernels, fused(): pl.pallas_call(functools.partial(kernel, planes), out_shape=jax.ShapeDtyp...  25.1 us
    unnamed x1, local copies, waits for them, and re-layouts  1.55 us

profile of v6, /device:TPU:0, one launch (start us, length us, event | category | flops | bytes accessed | tf_op | source)
XLA Modules:
  0.0 26.6 jit_solution(10584428063357525023)
XLA Ops:
  0.0 25.1 %shard_map.37 = bf16[448,128]{1,0:T(8,128)(2,1)} custom-call(bf16[128,256]{1,0:T(8,128)(2,1)} %tok_hbm.1, bf16[448,8192]{1,0:T(8,128)(2,1)} %bitcast.3, bf16[448,8192]{1,0:T(8,128)(2,1)} %bitcast.4), custom_call_target="tpu_custom_call" | custom-call | flops 1879048192 | bytes 14680064 | tf_op jit(solution)/shard_map/pallas_call | solution.py:200
  25.1 1.6 %copy.5 = bf16[128,448]{0,1:T(8,128)(2,1)} copy(bf16[128,448]{0,1:T(8,128)(2,1)} %bitcast.5) | data formatting | bytes 229376
